TPU v7x, 512 devices: a whole 4x8x8 slice. The times are simulated.
512 devices in a mesh: lvl: 16 (over z, core), fib: 32 (over y, x).
Axes of the slice: x: 4, y: 8, z: 8, core: 2. Of those that a mesh axis runs over, the one named last changes fastest.
Arguments:
- coefficients: float32 [256, 512, 1024], P('lvl', 'fib'), may hold values from -6 to 6
- local_vol: float32 [256, 512], P('lvl', 'fib'), may hold values from 0.1 to 0.6
Outputs:
- result: float32 [256, 512, 1024], P('lvl', 'fib')
All inputs are finite; a program needn't handle non-finite values.
Results may differ from a plain program's by a relative error of at most 0.00013.
Values sent between devices are 32-bit elements; how exact they have to be, the bound alone decides.
No kernel may reach another device: no remote copies, remote signals or barrier semaphores. Data moves between devices by JAX's collectives and lax.ppermute only.
A program may use at most 64 MiB of HBM per device.

v0:
```python
import jax
import jax.numpy as jnp
from jax import lax
from jax.sharding import PartitionSpec as P

KAPPA_SCALE = 8.0
DRIFT = 0.2
DISCOUNT = 0.05
EINSUM_DOWN = {0: "ij,jac->iac", 1: "ij,bjc->bic"}
EINSUM_UP = {0: "ji,jac->iac", 1: "ji,bjc->bic"}


def shifted(block, axis, distance):
    devices = range(lax.axis_size(axis))
    route = [(i - distance, i) for i in devices if i - distance in devices]
    return lax.ppermute(block, axis, route)


def lowest_power(index):
    return index & -index


def local_table(block):
    rows = jnp.arange(block, dtype=jnp.float32)[:, None]
    column_ids = jnp.arange(block + 1, dtype=jnp.int32)
    widths = jnp.where(
        (column_ids == 0) | (column_ids == block), block, lowest_power(column_ids)
    ).astype(jnp.float32)
    columns = column_ids.astype(jnp.float32)[None, :]
    return jnp.maximum(0.0, 1.0 - jnp.abs(rows - columns) / widths[None, :])


def along_shape(length, dim):
    shape = [1, 1, 1]
    shape[dim] = length
    return tuple(shape)


def coarse_row(point, length, count):
    members = jnp.arange(length, dtype=jnp.int32)
    widths = jnp.where(members == 0, count, lowest_power(members)).astype(jnp.float32)
    return jnp.maximum(0.0, 1.0 - jnp.abs(point - members.astype(jnp.float32)) / widths)


def coarse_column(index, length, count):
    members = jnp.arange(length, dtype=jnp.int32)
    own_width = jnp.where(index == 0, count, lowest_power(index)).astype(jnp.float32)
    distance = jnp.abs(members - index).astype(jnp.float32)
    return jnp.maximum(0.0, 1.0 - distance / own_width)


def fold_down_step(point, count, dim):

    def add_piece(carry, piece, start):
        length = piece.shape[dim]
        own = coarse_row(point, length, count).reshape(along_shape(length, dim))
        after = coarse_row(point + 1.0, length, count).reshape(along_shape(length, dim))
        return (
            jnp.sum(own * piece, axis=dim, keepdims=True),
            jnp.sum(after * piece, axis=dim, keepdims=True),
        )

    return add_piece


def fold_up_step(index, count, dim):

    def add_piece(carry, piece, start):
        length = piece.shape[dim]
        weight = coarse_column(index, length, count).reshape(along_shape(length, dim))
        return jnp.sum(weight * piece, axis=dim, keepdims=True)

    return add_piece


def fib_edge(values):
    return shifted(values, "fib", 1)


def fib_down(head, index, count):
    step_fn = fold_down_step(index.astype(jnp.float32), count, 1)
    start_pair = (jnp.zeros_like(head), jnp.zeros_like(head))
    return step_fn(start_pair, lax.all_gather(head, "fib", axis=1, tiled=True), jnp.int32(0))


def fib_up(dual, index, count):
    step_fn = fold_up_step(index, count, 1)
    return step_fn(
        jnp.zeros_like(dual), lax.all_gather(dual, "fib", axis=1, tiled=True), jnp.int32(0)
    )


def lvl_edge(values):
    return shifted(values, "lvl", 1)


def lvl_down(head, index, count):
    step_fn = fold_down_step(index.astype(jnp.float32), count, 0)
    start_pair = (jnp.zeros_like(head), jnp.zeros_like(head))
    return step_fn(start_pair, lax.all_gather(head, "lvl", axis=0, tiled=True), jnp.int32(0))


def lvl_up(dual, index, count):
    step_fn = fold_up_step(index, count, 0)
    return step_fn(
        jnp.zeros_like(dual), lax.all_gather(dual, "lvl", axis=0, tiled=True), jnp.int32(0)
    )


def apply_pass(values, sigma, dim, index, count, moves):
    down_move, edge_move, up_move = moves
    block = values.shape[dim]
    total = block * count
    head = lax.slice_in_dim(values, 0, 1, axis=dim)
    own_node, next_node = down_move(head, index, count)
    extended = jnp.concatenate(
        [own_node, lax.slice_in_dim(values, 1, block, axis=dim), next_node], axis=dim
    )
    table = local_table(block)
    nodal = jnp.einsum(EINSUM_DOWN[dim], table, extended, precision=lax.Precision.HIGHEST)
    below_row = edge_move(lax.slice_in_dim(nodal, block - 1, block, axis=dim))
    below = jnp.concatenate([below_row, lax.slice_in_dim(nodal, 0, block - 1, axis=dim)], axis=dim)
    above = jnp.concatenate([lax.slice_in_dim(nodal, 1, block, axis=dim), next_node], axis=dim)
    position = (index * block + jnp.arange(block, dtype=jnp.int32)).astype(jnp.float32) / total
    place = position.reshape(along_shape(block, dim))
    kappa = KAPPA_SCALE * 0.5 * sigma * sigma * place * place
    beta = DRIFT * place
    image = (
        (2.0 / 3.0 + 2.0 * kappa + DISCOUNT) * nodal
        + (1.0 / 6.0 - kappa + beta) * below
        + (1.0 / 6.0 - kappa - beta) * above
    )
    moment = jnp.einsum(EINSUM_UP[dim], table, image, precision=lax.Precision.HIGHEST)
    left_part = lax.slice_in_dim(moment, 0, 1, axis=dim)
    right_part = lax.slice_in_dim(moment, block, block + 1, axis=dim)
    dual = left_part + edge_move(right_part)
    coarse = up_move(dual, index, count)
    coarse_width = jnp.where(index == 0, total, block * lowest_power(index)).astype(jnp.float32)
    fine_ids = jnp.arange(1, block, dtype=jnp.int32)
    fine_width = lowest_power(fine_ids).astype(jnp.float32).reshape(along_shape(block - 1, dim))
    fine = lax.slice_in_dim(moment, 1, block, axis=dim) / fine_width
    return jnp.concatenate([coarse / coarse_width, fine], axis=dim)


def per_device(coefficients, local_vol):
    sigma = local_vol[:, :, None]
    fib_index = lax.axis_index("fib")
    fib_count = lax.axis_size("fib")
    after_a = apply_pass(coefficients, sigma, 1, fib_index, fib_count, (fib_down, fib_edge, fib_up))
    lvl_index = lax.axis_index("lvl")
    lvl_count = lax.axis_size("lvl")
    return apply_pass(after_a, sigma, 0, lvl_index, lvl_count, (lvl_down, lvl_edge, lvl_up))


def solution(mesh):
    placed = (P("lvl", "fib", None), P("lvl", "fib"))
    return jax.shard_map(
        per_device, mesh=mesh, in_specs=placed, out_specs=P("lvl", "fib", None), check_vma=False
    )
```

profile of v0, /device:TPU:1, one launch (start us, length us, event | category | flops | bytes accessed | tf_op | source)
XLA Modules:
  0.0 316.4 jit_solution(6241878897389079636)
XLA Ops:
  6.5 1.1 slice.48
  7.6 0.6 copy.18
  8.3 0.0 all-gather.5.cloned.1.call-update
  8.3 0.0 all-gather.7.cloned.1.call-start
  8.4 1.3 slice.49
  9.8 0.1 subtract_add_fusion
  9.9 85.7 %all-gather.5.cloned.1.call-done = f32[16,32,1024]{2,0,1:T(8,128)} async-done(((f32[16,1,1024]{2,0,1:T(8,128)}), f32[16,32,1024]{2,0,1:T(8,128)}) %all-gather.5.cloned.1.call-update) | async-done | bytes 2097168 | tf_op jit(solution)/shard_map/all_gather | solution.py:83
  95.6 1.9 multiply_reduce_fusion.2
  97.6 1.5 fusion.8
  99.2 0.1 slice.64
  99.3 1.9 collective-permute-start
  101.2 0.2 fusion.57
  101.4 1.1 collective-permute-done
  102.5 1.9 convolution_bitcast_fusion
  104.5 3.7 %collective-permute-start.1 = (f32[16,1,1024]{2,1,0:T(1,128)S(1)}, f32[16,1,1024]{2,1,0:T(1,128)S(1)}, u32[]{:S(2)}, u32[]{:S(2)}) collective-permute-start(f32[16,1,1024]{2,1,0:T(1,128)S(1)} %slice.68), channel_id=1, source_target_pairs={{0,1},{1,2},{2,3},{3,4},{4,5},{5,6},{6,7},{7,8},{8,9},{9,10},{10,1... | collective-permute-start | bytes 196616 | tf_op jit(solution)/shard_map/ppermute | solution.py:16
  108.2 1.3 collective-permute-done.1
  109.5 0.1 slice_add_fusion.1
  109.6 0.6 copy.11
  110.2 0.0 all-gather.7.cloned.1.call-update
  110.2 0.0 all-gather.9.cloned.1.call-start
  110.3 0.3 slice_divide_fusion.1
  110.6 90.1 %all-gather.7.cloned.1.call-done = f32[16,32,1024]{2,0,1:T(8,128)} async-done(((f32[16,1,1024]{2,0,1:T(8,128)}), f32[16,32,1024]{2,0,1:T(8,128)}) %all-gather.7.cloned.1.call-update) | async-done | bytes 2097168 | tf_op jit(solution)/shard_map/all_gather | solution.py:89
  200.7 1.8 multiply_reduce_fusion
  202.6 0.6 pad_maximum_fusion.1
  203.3 0.0 all-gather.11.cloned.1.call-start
  203.3 0.1 copy.13
  203.4 0.1 copy.14
  203.4 0.1 copy.9
  203.5 43.4 %all-gather.9.cloned.1.call-done = f32[16,16,1024]{2,1,0:T(8,128)} async-done(((f32[1,16,1024]{2,1,0:T(8,128)}), f32[16,16,1024]{2,1,0:T(8,128)}) %all-gather.9.cloned.1.call-update) | async-done | bytes 1048592 | tf_op jit(solution)/shard_map/all_gather | solution.py:100
  247.0 1.4 multiply_reduce_fusion.5
  248.4 0.2 fusion.12
  248.6 1.6 fusion.6
  250.3 0.1 slice.70
  250.3 2.4 collective-permute-start.2
  252.8 0.2 fusion.56
  253.0 0.1 copy.15
  253.1 1.0 collective-permute-done.2
  254.1 1.7 fusion.23
  255.8 4.3 %collective-permute-start.3 = (f32[1,16,1024]{2,0,1:T(1,128)S(1)}, f32[1,16,1024]{2,0,1:T(1,128)S(1)}, u32[]{:S(2)}, u32[]{:S(2)}) collective-permute-start(f32[1,16,1024]{2,0,1:T(1,128)S(1)} %slice.74), channel_id=1, source_target_pairs={{0,32},{32,64},{64,96},{96,128},{128,160},{160,192},{192,224},{224... | collective-permute-start | bytes 196616 | tf_op jit(solution)/shard_map/ppermute | solution.py:16
  260.1 1.3 collective-permute-done.3
  261.4 0.1 slice_add_fusion
  261.5 0.6 copy.16
  262.1 0.0 all-gather.11.cloned.1.call-update
  262.2 0.3 slice_divide_fusion
  262.4 44.2 %all-gather.11.cloned.1.call-done = f32[16,16,1024]{2,1,0:T(8,128)} async-done(((f32[1,16,1024]{2,1,0:T(8,128)}), f32[16,16,1024]{2,1,0:T(8,128)}) %all-gather.11.cloned.1.call-update) | async-done | bytes 1048592 | tf_op jit(solution)/shard_map/all_gather | solution.py:106
  306.6 1.4 multiply_reduce_fusion.3
  308.0 0.2 pad_maximum_fusion
  308.3 1.6 copy.17
  (20 shorter events, 0.4 us)
Async XLA Ops:
  6.5 3.2 %copy-start = (f32[16,16]{1,0:T(8,128)S(1)}, f32[16,16]{1,0:T(8,128)}, u32[]{:S(2)}) copy-start(f32[16,16]{1,0:T(8,128)} %param.3) | copy-start | bytes 3076
  6.5 89.0 %all-gather.5.cloned.1.call-start = ((), (), s32[]{:S(2)}) async-start(), calls=%async_computation | async-start | bytes 2162688 | tf_op jit(solution)/shard_map/all_gather | solution.py:83
  8.3 192.4 %all-gather.7.cloned.1.call-start = ((), (), s32[]{:S(2)}) async-start(), calls=%async_computation.1 | async-start | bytes 2162688 | tf_op jit(solution)/shard_map/all_gather | solution.py:89
  99.3 3.2 %collective-permute-start = (f32[16,1,1024]{2,1,0:T(1,128)S(1)}, f32[16,1,1024]{2,1,0:T(1,128)S(1)}, u32[]{:S(2)}, u32[]{:S(2)}) collective-permute-start(f32[16,1,1024]{2,1,0:T(1,128)S(1)} %slice.64), channel_id=1, source_target_pairs={{0,1},{1,2},{2,3},{3,4},{4,5},{5,6},{6,7},{7,8},{8,9},{9,10},{10,1... | collective-permute-start | bytes 196616 | tf_op jit(solution)/shard_map/ppermute | solution.py:16
  104.5 5.0 %collective-permute-start.1 = (f32[16,1,1024]{2,1,0:T(1,128)S(1)}, f32[16,1,1024]{2,1,0:T(1,128)S(1)}, u32[]{:S(2)}, u32[]{:S(2)}) collective-permute-start(f32[16,1,1024]{2,1,0:T(1,128)S(1)} %slice.68), channel_id=1, source_target_pairs={{0,1},{1,2},{2,3},{3,4},{4,5},{5,6},{6,7},{7,8},{8,9},{9,10},{10,1... | collective-permute-start | bytes 196616 | tf_op jit(solution)/shard_map/ppermute | solution.py:16
  110.2 136.7 %all-gather.9.cloned.1.call-start = ((), (), s32[]{:S(2)}) async-start(), calls=%async_computation.2 | async-start | bytes 1114112 | tf_op jit(solution)/shard_map/all_gather | solution.py:100
  203.3 103.3 %all-gather.11.cloned.1.call-start = ((), (), s32[]{:S(2)}) async-start(), calls=%async_computation.3 | async-start | bytes 1114112 | tf_op jit(solution)/shard_map/all_gather | solution.py:106
  250.3 3.8 %collective-permute-start.2 = (f32[1,16,1024]{2,0,1:T(1,128)S(1)}, f32[1,16,1024]{2,0,1:T(1,128)S(1)}, u32[]{:S(2)}, u32[]{:S(2)}) collective-permute-start(f32[1,16,1024]{2,0,1:T(1,128)S(1)} %slice.70), channel_id=1, source_target_pairs={{0,32},{32,64},{64,96},{96,128},{128,160},{160,192},{192,224},{224... | collective-permute-start | bytes 196616 | tf_op jit(solution)/shard_map/ppermute | solution.py:16
  255.8 5.6 %collective-permute-start.3 = (f32[1,16,1024]{2,0,1:T(1,128)S(1)}, f32[1,16,1024]{2,0,1:T(1,128)S(1)}, u32[]{:S(2)}, u32[]{:S(2)}) collective-permute-start(f32[1,16,1024]{2,0,1:T(1,128)S(1)} %slice.74), channel_id=1, source_target_pairs={{0,32},{32,64},{64,96},{96,128},{128,160},{160,192},{192,224},{224... | collective-permute-start | bytes 196616 | tf_op jit(solution)/shard_map/ppermute | solution.py:16
Sparse Core Ops, SparseCore 0:
  10.5 85.0 all-gather.4
  110.3 90.3 all-gather.6
  203.4 43.5 all-gather.8
  262.2 44.3 all-gather.10
where the time goes:
time: 317 us; the launch traced here: 316 us
  waiting for transfers between devices  268 us (85%)
  between operations  13.5 us (4%)
  starting transfers between devices  12.5 us (4%)
  other arithmetic  8.45 us (3%)
  local copies, waits for them, and re-layouts  7.02 us (2%)
  matrix products  6.73 us (2%)
    all_gather x1, waiting for transfers between devices, fib_up(): lax.all_gather(dual, 'fib', axis=1, tiled=True)  90.1 us
    all_gather x1, waiting for transfers between devices, fib_down(): lax.all_gather(head, 'fib', axis=1, tiled=True)  85.7 us
    all_gather x1, waiting for transfers between devices, lvl_up(): lax.all_gather(dual, 'lvl', axis=0, tiled=True)  44.2 us
    all_gather x1, waiting for transfers between devices, lvl_down(): lax.all_gather(head, 'lvl', axis=0, tiled=True)  43.4 us
    ppermute x4, starting transfers between devices, shifted(): return lax.ppermute(block, axis, route)  12.3 us
  transfers between devices with their start and end apart: 8, of which 8 were waited for; matrix products, arithmetic and copies ran while one was open for 1% of the time, Pallas kernels for 0%

commit v1 on v0

v1 whole, which is shorter than its diff:
```python
import functools

import jax
import jax.numpy as jnp
from jax import lax
from jax.experimental import pallas as pl
from jax.experimental.pallas import tpu as pltpu
from jax.sharding import PartitionSpec as P

KAPPA_SCALE = 8.0
DRIFT = 0.2
DISCOUNT = 0.05
CENTRE = 2.0 / 3.0 + DISCOUNT
SIDE = 1.0 / 6.0
LINEAR = CENTRE + 2.0 * SIDE
LANES = 128
VMEM_LIMIT = 32 * 1024 * 1024


def descend(rows, low, high):
    n = len(rows)
    nodal = [low] + [None] * (n - 1) + [high]
    step = n // 2
    while step >= 1:
        for at in range(step, n, 2 * step):
            left, right = nodal[at - step], nodal[at + step]
            if left is None and right is None:
                nodal[at] = rows[at]
            elif left is None or right is None:
                nodal[at] = rows[at] + 0.5 * (right if left is None else left)
            else:
                nodal[at] = rows[at] + 0.5 * (left + right)
        step //= 2
    return nodal


def add(a, b):
    if a is None:
        return b
    return a if b is None else a + b


def ascend(rows):
    n = len(rows)
    sums = list(rows) + [None]
    step = 1
    while step < n:
        for at in range(step, n, 2 * step):
            half = 0.5 * sums[at]
            sums[at - step] = add(sums[at - step], half)
            sums[at + step] = add(sums[at + step], half)
        step *= 2
    return sums


def lowest(index):
    return index & -index


def local_pass(rows, kappas, first_beta, total):
    n = len(rows)
    nodal = descend(rows, None, None)
    images = []
    for at in range(n):
        beta = first_beta + DRIFT * at / total
        kappa = kappas(at)
        above = nodal[at + 1]
        if at == 0:
            images.append((SIDE - beta - kappa) * above)
            continue
        below = nodal[at - 1]
        middle = nodal[at]
        image = (CENTRE + 2.0 * kappa) * middle
        if below is not None:
            image = image + (SIDE + beta - kappa) * below
        if above is not None:
            image = image + (SIDE - beta - kappa) * above
        images.append(image)
    sums = ascend(images)
    fine = [sums[at] * (1.0 / lowest(at)) for at in range(1, n)]
    return fine, (rows[0], sums[0], sums[n], nodal[n - 1])


def end_weights(at, n, first_beta, total):
    tilt = (first_beta + DRIFT * at / total) * (2.0 / n)
    return LINEAR * (1.0 - at / n) + tilt, LINEAR * (at / n) - tilt


def coarse_pass(heads, lefts, rights, lasts, kappas, n):
    count = len(heads)
    total = n * count
    inner = descend([None] + heads[1:], heads[0], None)
    node = inner[:count]
    share = [r / n for r in range(n)]
    left0 = sum(1 - s for s in share[1:])
    left1 = sum((1 - s) ** 2 for s in share[1:])
    left2 = sum((1 - s) * s for s in share[1:])
    left3 = sum((1 - s) * s * n for s in share[1:])
    right0 = sum(share[1:])
    right1 = left2
    right2 = sum(s * s for s in share[1:])
    right3 = sum(s * s * n for s in share[1:])
    slope = DRIFT / total
    duals = []
    for i in range(count):
        beta = DRIFT * i / count
        kappa = kappas[i]
        tilt = (2.0 / n) * (beta * left0 + slope * left3)
        following = node[i + 1] if i + 1 < count else None
        upper = SIDE - beta - kappa
        own = CENTRE + 2.0 * kappa + upper * (1.0 - 1.0 / n) + (LINEAR * left1 + tilt)
        dual = lefts[i]
        if following is not None:
            dual = dual + (upper * (1.0 / n) + (LINEAR * left2 - tilt)) * following
        if i > 0:
            before_beta = DRIFT * (i - 1) / count
            tilt = (2.0 / n) * (before_beta * right0 + slope * right3)
            lower = SIDE + beta - kappa
            own = own + lower * (1.0 - 1.0 / n) + (LINEAR * right2 - tilt)
            dual = dual + rights[i - 1] + lower * lasts[i - 1]
            dual = dual + (lower * (1.0 / n) + (LINEAR * right1 + tilt)) * node[i - 1]
        duals.append(dual + own * node[i])
    sums = ascend(duals)
    outs = [sums[i] * (1.0 / (total if i == 0 else n * lowest(i))) for i in range(count)]
    return node, outs


def first_kernel(count, values_ref, vol_ref, packet_ref, fine_ref, kappa_ref):
    nb, n, cols = values_ref.shape
    tiles = cols // LANES
    total = n * count
    index = lax.axis_index("fib").astype(jnp.float32)
    first_beta = index * (DRIFT / count)
    vol = vol_ref[...]
    for r in range(n):
        place = index * (1.0 / count) + r / total
        root = vol[:, r : r + 1] * place
        kappa_ref[r] = jnp.broadcast_to((KAPPA_SCALE * 0.5) * root * root, (nb, LANES))
    parts = count // nb
    per = tiles // parts
    rows = 4 * per + 1
    stride = parts * rows
    for part in range(parts):
        packet_ref[pl.ds(part * rows + rows - 1, nb, stride=stride), :] = kappa_ref[0]
    for t in range(tiles):
        lanes = slice(t * LANES, (t + 1) * LANES)
        block = jnp.swapaxes(values_ref[:, :, lanes], 0, 1)
        fine, quads = local_pass([block[r] for r in range(n)], lambda r: kappa_ref[r], first_beta, total)
        zero = jnp.zeros_like(fine[0])
        fine_ref[:, :, lanes] = jnp.swapaxes(jnp.stack([zero] + fine), 0, 1)
        for q, quad in enumerate(quads):
            start = (t // per) * rows + q * per + t % per
            packet_ref[pl.ds(start, nb, stride=stride), :] = quad


def coarse_kernel(count, n, per, packet_ref, answer_ref):
    rows = 4 * per + 1

    def piece(i, q):
        return packet_ref[i * rows + q * per : i * rows + (q + 1) * per, :]

    quads = [[piece(i, q) for i in range(count)] for q in range(4)]
    kappas = [packet_ref[(i + 1) * rows - 1 : (i + 1) * rows, :] for i in range(count)]
    node, outs = coarse_pass(*quads, kappas, n)
    for i in range(count):
        base = 3 * per * i
        answer_ref[base : base + per, :] = node[i]
        answer_ref[base + per : base + 2 * per, :] = (
            node[i + 1] if i + 1 < count else jnp.zeros_like(node[i])
        )
        answer_ref[base + 2 * per : base + 3 * per, :] = outs[i]


def second_kernel(fib_count, lvl_count, answer_ref, fine_ref, vol_ref, packet_ref, next_ref, kappa_ref):
    n, na, cols = fine_ref.shape
    tiles = cols // LANES
    fib_total = na * fib_count
    total = n * lvl_count
    fib_beta = lax.axis_index("fib").astype(jnp.float32) * (DRIFT / fib_count)
    index = lax.axis_index("lvl").astype(jnp.float32)
    first_beta = index * (DRIFT / lvl_count)
    vol = vol_ref[...]
    diagonal = lax.broadcasted_iota(jnp.int32, (na, na), 0) == lax.broadcasted_iota(
        jnp.int32, (na, na), 1
    )
    for r in range(n):
        place = index * (1.0 / lvl_count) + r / total
        column = jnp.sum(jnp.where(diagonal, vol[r : r + 1, :], 0.0), axis=1, keepdims=True)
        root = column * place
        kappa_ref[r] = jnp.broadcast_to((KAPPA_SCALE * 0.5) * root * root, (na, LANES))
    at = lax.broadcasted_iota(jnp.int32, (na, LANES), 0)
    tilt = (fib_beta + at.astype(jnp.float32) * (DRIFT / fib_total)) * (2.0 / na)
    share = at.astype(jnp.float32) * (1.0 / na)
    is_head = at == 0
    low = LINEAR * (1.0 - share) + tilt
    high = LINEAR * share - tilt
    parts = fib_count // n
    per = tiles // parts
    rows = 4 * tiles + 1
    packet_ref[pl.ds(rows - 1, na, stride=rows), :] = kappa_ref[0]
    for t in range(tiles):
        lanes = slice(t * LANES, (t + 1) * LANES)
        block = []
        for b in range(n):
            base = (b * parts + t // per) * 3 * per + t % per
            own = answer_ref[base : base + 1, :]
            following = answer_ref[base + per : base + per + 1, :]
            head = answer_ref[base + 2 * per : base + 2 * per + 1, :]
            body = fine_ref[b, :, lanes] + low * own + high * following
            block.append(jnp.where(is_head, head, body))
        fine, quads = local_pass(block, lambda r: kappa_ref[r], first_beta, total)
        for r in range(1, n):
            next_ref[r, :, lanes] = fine[r - 1]
        for q, quad in enumerate(quads):
            packet_ref[pl.ds(q * tiles + t, na, stride=rows), :] = quad


def last_kernel(count, answer_ref, fine_ref, out_ref):
    n, na, cols = fine_ref.shape
    tiles = cols // LANES
    total = n * count
    first_beta = lax.axis_index("lvl").astype(jnp.float32) * (DRIFT / count)
    for t in range(tiles):
        lanes = slice(t * LANES, (t + 1) * LANES)
        own, following, head = (
            answer_ref[pl.ds(q * tiles + t, na, stride=3 * tiles), :] for q in range(3)
        )
        out_ref[0, :, lanes] = head
        for r in range(1, n):
            low, high = end_weights(r, n, first_beta, total)
            out_ref[r, :, lanes] = fine_ref[r, :, lanes] + low * own + high * following


def whole(count):
    return [pl.BlockSpec(memory_space=pltpu.VMEM)] * count


def call(body, name, inputs, outs, scratch=()):
    return pl.pallas_call(
        body,
        name=name,
        out_shape=[jax.ShapeDtypeStruct(shape, jnp.float32) for shape in outs],
        in_specs=whole(len(inputs)),
        out_specs=whole(len(outs)),
        scratch_shapes=[pltpu.VMEM(shape, jnp.float32) for shape in scratch],
        compiler_params=pltpu.CompilerParams(vmem_limit_bytes=VMEM_LIMIT),
    )(*inputs)


def swap(packets, axis, count):
    apart = packets.reshape(count, packets.shape[0] // count, 1, LANES)
    return lax.all_to_all(apart, axis, 0, 0).reshape(packets.shape)


def per_device(coefficients, local_vol):
    nb, na, cols = coefficients.shape
    fibs, lvls = lax.axis_size("fib"), lax.axis_size("lvl")
    tiles = cols // LANES
    per = tiles * nb // fibs
    packets, fine = call(
        functools.partial(first_kernel, fibs),
        "first",
        (coefficients, local_vol),
        ((fibs * (4 * per + 1), LANES), (nb, na, cols)),
        ((na, nb, LANES),),
    )
    packets = swap(packets, "fib", fibs)
    (answers,) = call(
        functools.partial(coarse_kernel, fibs, na, per), "coarse_a", (packets,), ((fibs * 3 * per, LANES),)
    )
    answers = swap(answers, "fib", fibs)
    packets, fine = call(
        functools.partial(second_kernel, fibs, lvls),
        "second",
        (answers, fine, local_vol),
        ((lvls * (4 * tiles + 1), LANES), (nb, na, cols)),
        ((nb, na, LANES),),
    )
    packets = swap(packets, "lvl", lvls)
    (answers,) = call(
        functools.partial(coarse_kernel, lvls, nb, tiles), "coarse_b", (packets,), ((lvls * 3 * tiles, LANES),)
    )
    answers = swap(answers, "lvl", lvls)
    (out,) = call(functools.partial(last_kernel, lvls), "last", (answers, fine), ((nb, na, cols),))
    return out


def solution(mesh):
    placed = (P("lvl", "fib", None), P("lvl", "fib"))
    return jax.shard_map(
        per_device, mesh=mesh, in_specs=placed, out_specs=P("lvl", "fib", None), check_vma=False
    )
```

time: 317 us -> 79.5 us (0.25)
  waiting for transfers between devices: 268 us -> 0 us
  blocking collectives: 0 us -> 74.5 us
  between operations: 13.5 us -> 0.02 us
  starting transfers between devices: 12.5 us -> 0 us
  other arithmetic: 8.45 us -> 0 us
  matrix products: 6.73 us -> 0 us
  local copies, waits for them, and re-layouts: 7.02 us -> 1.92 us
    all_gather x4 -> x0, waiting for transfers between devices: 263 us -> none  [the longest x1 90.1 us: fib_up(): lax.all_gather(dual, 'fib', axis=1, tiled=True)]
    all_to_all x0 -> x4, blocking collectives: none -> 74.5 us  [swap(): return lax.all_to_all(apart, axis, 0, 0).reshape(packets.shape)]
    ppermute x4 -> x0, starting transfers between devices: 12.3 us -> none  [shifted(): return lax.ppermute(block, axis, route)]
    dot_general x4 -> x0, matrix products: 6.73 us -> none  [the longest x2 3.56 us: apply_pass(): jnp.einsum(EINSUM_UP[dim], table, image, precision=lax.Precision.HIGHEST)]
    reduce_sum x4 -> x0, other arithmetic: 6.56 us -> none  [the longest x2 3.4 us: add_piece(): jnp.sum(own * piece, axis=dim, keepdims=True)]
    ppermute x4 -> x0, waiting for transfers between devices: 4.74 us -> none  [shifted(): return lax.ppermute(block, axis, route)]
  transfers between devices with their start and end apart: 8 -> 0, of which waited for: 8 -> 0; matrix products, arithmetic and copies ran while one was open for 1% -> 0% of each run, Pallas kernels for 0% -> 0%
where the time goes in v1:
time: 79.5 us; the launch traced here: 79.2 us
  blocking collectives  74.5 us (94%)
  Pallas kernels  2.72 us (3%)
  local copies, waits for them, and re-layouts  1.92 us (2%)
    all_to_all x4, blocking collectives, swap(): return lax.all_to_all(apart, axis, 0, 0).reshape(packets.shape)  74.5 us
    pallas_call x5, Pallas kernels, call(): pl.pallas_call(body, name=name, out_shape=[jax.ShapeDtypeStruct(shape, jn...  2.72 us
    unnamed x4, local copies, waits for them, and re-layouts  1.92 us

profile of v1, /device:TPU:1, one launch (start us, length us, event | category | flops | bytes accessed | tf_op | source)
XLA Modules:
  0.0 79.2 jit_solution(16088758896551708945)
XLA Ops:
  0.0 0.0 copy-start
  0.0 1.2 %copy-done = f32[16,16,1024]{2,1,0:T(8,128)S(1)} copy-done((f32[16,16,1024]{2,1,0:T(8,128)S(1)}, f32[16,16,1024]{2,1,0:T(8,128)}, u32[]{:S(2)}) %copy-start) | copy-done | bytes 1048600
  1.2 0.0 copy-start.1
  1.2 0.7 copy-done.1
  1.9 0.7 first.1
  2.7 22.1 %all_to_all.20 = f32[32,17,1,128]{3,2,1,0:T(1,128)S(1)} all-to-all(f32[32,17,1,128]{3,2,1,0:T(1,128)S(1)} %bitcast.16), channel_id=1, replica_groups=mesh['lvl'=16,'fib'=32] {'fib'}, dimensions={0} | all-to-all | bytes 557056 | tf_op jit(solution)/shard_map/all_to_all | solution.py:252
  24.8 0.2 coarse_a.1
  25.0 14.1 %all_to_all.21 = f32[32,12,1,128]{3,2,1,0:T(1,128)S(1)} all-to-all(f32[32,12,1,128]{3,2,1,0:T(1,128)S(1)} %bitcast.15), channel_id=1, replica_groups=mesh['lvl'=16,'fib'=32] {'fib'}, dimensions={0} | all-to-all | bytes 393216 | tf_op jit(solution)/shard_map/all_to_all | solution.py:252
  39.1 0.6 second.1
  39.7 25.2 %all_to_all.22 = f32[16,33,1,128]{3,2,1,0:T(1,128)S(1)} all-to-all(f32[16,33,1,128]{3,2,1,0:T(1,128)S(1)} %bitcast.17), channel_id=1, replica_groups=mesh['lvl'=16,'fib'=32] {'lvl'}, dimensions={0} | all-to-all | bytes 540672 | tf_op jit(solution)/shard_map/all_to_all | solution.py:252
  64.9 0.1 coarse_b.1
  65.0 13.0 %all_to_all.23 = f32[16,24,1,128]{3,1,2,0:T(8,128)S(1)} all-to-all(f32[16,24,1,128]{3,1,2,0:T(8,128)S(1)} %bitcast.14), channel_id=1, replica_groups=mesh['lvl'=16,'fib'=32] {'lvl'}, dimensions={0} | all-to-all | bytes 393216 | tf_op jit(solution)/shard_map/all_to_all | solution.py:252
  78.0 1.2 %last.1 = f32[16,16,1024]{2,1,0:T(8,128)} custom-call(f32[384,128]{1,0:T(8,128)S(1)} %bitcast.13, f32[16,16,1024]{2,1,0:T(8,128)S(1)} %get-tuple-element.12.fine_ref), custom_call_target="tpu_custom_call" | custom-call | tf_op jit(solution)/shard_map/last/pallas_call | solution.py:239
Async XLA Ops:
  0.0 1.2 %copy-start = (f32[16,16,1024]{2,1,0:T(8,128)S(1)}, f32[16,16,1024]{2,1,0:T(8,128)}, u32[]{:S(2)}) copy-start(f32[16,16,1024]{2,1,0:T(8,128)} %values_ref.1) | copy-start | bytes 3145732
  1.2 0.7 copy-start.1

commit v2 on v1

--- a/solution.py
+++ b/solution.py
@@ -14,6 +14,7 @@
 SIDE = 1.0 / 6.0
 LINEAR = CENTRE + 2.0 * SIDE
 LANES = 128
+CHUNKS = 4
 VMEM_LIMIT = 32 * 1024 * 1024
 
 
@@ -125,13 +126,25 @@
     return node, outs
 
 
-def first_kernel(count, values_ref, vol_ref, packet_ref, fine_ref, kappa_ref):
+def first_kernel(count, values_ref, vol_ref, packet_ref, fine_ref, kappa_ref, stage_ref, own_vol_ref, sems):
     nb, n, cols = values_ref.shape
     tiles = cols // LANES
     total = n * count
+    chunks, _, _, width = stage_ref.shape
+    vol_copy = pltpu.make_async_copy(vol_ref, own_vol_ref, sems.at[chunks])
+    vol_copy.start()
+    copies = []
+    for chunk in range(chunks):
+        copies.append(
+            pltpu.make_async_copy(
+                values_ref.at[:, :, pl.ds(chunk * width, width)], stage_ref.at[chunk], sems.at[chunk]
+            )
+        )
+        copies[-1].start()
     index = lax.axis_index("fib").astype(jnp.float32)
     first_beta = index * (DRIFT / count)
-    vol = vol_ref[...]
+    vol_copy.wait()
+    vol = own_vol_ref[...]
     for r in range(n):
         place = index * (1.0 / count) + r / total
         root = vol[:, r : r + 1] * place
@@ -143,11 +156,13 @@
     for part in range(parts):
         packet_ref[pl.ds(part * rows + rows - 1, nb, stride=stride), :] = kappa_ref[0]
     for t in range(tiles):
-        lanes = slice(t * LANES, (t + 1) * LANES)
-        block = jnp.swapaxes(values_ref[:, :, lanes], 0, 1)
-        fine, quads = local_pass([block[r] for r in range(n)], lambda r: kappa_ref[r], first_beta, total)
-        zero = jnp.zeros_like(fine[0])
-        fine_ref[:, :, lanes] = jnp.swapaxes(jnp.stack([zero] + fine), 0, 1)
+        copies[t].wait()
+        tile = stage_ref.at[t].reshape(nb * n, LANES)
+        block = [tile[pl.ds(r, nb, stride=n), :] for r in range(n)]
+        fine, quads = local_pass(block, lambda r: kappa_ref[r], first_beta, total)
+        fine_ref[t, pl.ds(0, nb, stride=n), :] = jnp.zeros_like(fine[0])
+        for r in range(1, n):
+            fine_ref[t, pl.ds(r, nb, stride=n), :] = fine[r - 1]
         for q, quad in enumerate(quads):
             start = (t // per) * rows + q * per + t % per
             packet_ref[pl.ds(start, nb, stride=stride), :] = quad
@@ -172,8 +187,8 @@
 
 
 def second_kernel(fib_count, lvl_count, answer_ref, fine_ref, vol_ref, packet_ref, next_ref, kappa_ref):
-    n, na, cols = fine_ref.shape
-    tiles = cols // LANES
+    n, na, _ = next_ref.shape
+    tiles = fine_ref.shape[0]
     fib_total = na * fib_count
     total = n * lvl_count
     fib_beta = lax.axis_index("fib").astype(jnp.float32) * (DRIFT / fib_count)
@@ -206,7 +221,7 @@
             own = answer_ref[base : base + 1, :]
             following = answer_ref[base + per : base + per + 1, :]
             head = answer_ref[base + 2 * per : base + 2 * per + 1, :]
-            body = fine_ref[b, :, lanes] + low * own + high * following
+            body = fine_ref[t, b * na : (b + 1) * na, :] + low * own + high * following
             block.append(jnp.where(is_head, head, body))
         fine, quads = local_pass(block, lambda r: kappa_ref[r], first_beta, total)
         for r in range(1, n):
@@ -215,36 +230,50 @@
             packet_ref[pl.ds(q * tiles + t, na, stride=rows), :] = quad
 
 
-def last_kernel(count, answer_ref, fine_ref, out_ref):
+def last_kernel(count, answer_ref, fine_ref, out_ref, stage_ref, sems):
     n, na, cols = fine_ref.shape
     tiles = cols // LANES
     total = n * count
     first_beta = lax.axis_index("lvl").astype(jnp.float32) * (DRIFT / count)
-    for t in range(tiles):
-        lanes = slice(t * LANES, (t + 1) * LANES)
-        own, following, head = (
-            answer_ref[pl.ds(q * tiles + t, na, stride=3 * tiles), :] for q in range(3)
+    chunks, deep = stage_ref.shape[:2]
+    copies = []
+    for chunk in range(chunks):
+        for t in range(tiles):
+            lanes = slice(t * LANES, (t + 1) * LANES)
+            own, following, head = (
+                answer_ref[pl.ds(q * tiles + t, na, stride=3 * tiles), :] for q in range(3)
+            )
+            for at in range(deep):
+                r = chunk * deep + at
+                if r == 0:
+                    stage_ref[chunk, at, :, lanes] = head
+                    continue
+                low, high = end_weights(r, n, first_beta, total)
+                stage_ref[chunk, at, :, lanes] = fine_ref[r, :, lanes] + low * own + high * following
+        copies.append(
+            pltpu.make_async_copy(
+                stage_ref.at[chunk], out_ref.at[pl.ds(chunk * deep, deep)], sems.at[chunk]
+            )
         )
-        out_ref[0, :, lanes] = head
-        for r in range(1, n):
-            low, high = end_weights(r, n, first_beta, total)
-            out_ref[r, :, lanes] = fine_ref[r, :, lanes] + low * own + high * following
-
-
-def whole(count):
-    return [pl.BlockSpec(memory_space=pltpu.VMEM)] * count
-
-
-def call(body, name, inputs, outs, scratch=()):
+        copies[-1].start()
+    for copy in copies:
+        copy.wait()
+
+
+def call(body, name, inputs, outs, scratch=(), copies=0, far_in=(), far_out=()):
+    near, far = pl.BlockSpec(memory_space=pltpu.VMEM), pl.BlockSpec(memory_space=pltpu.HBM)
+    rooms = [pltpu.VMEM(shape, jnp.float32) for shape in scratch]
+    if copies:
+        rooms.append(pltpu.SemaphoreType.DMA((copies,)))
     return pl.pallas_call(
         body,
         name=name,
         out_shape=[jax.ShapeDtypeStruct(shape, jnp.float32) for shape in outs],
-        in_specs=whole(len(inputs)),
-        out_specs=whole(len(outs)),
-        scratch_shapes=[pltpu.VMEM(shape, jnp.float32) for shape in scratch],
+        in_specs=[far if i in far_in else near for i in range(len(inputs))],
+        out_specs=[far if i in far_out else near for i in range(len(outs))],
+        scratch_shapes=rooms,
         compiler_params=pltpu.CompilerParams(vmem_limit_bytes=VMEM_LIMIT),
-    )(*inputs)
+    )(*(pltpu.with_memory_space_constraint(x, pltpu.HBM) if i in far_in else x for i, x in enumerate(inputs)))
 
 
 def swap(packets, axis, count):
@@ -261,8 +290,10 @@
         functools.partial(first_kernel, fibs),
         "first",
         (coefficients, local_vol),
-        ((fibs * (4 * per + 1), LANES), (nb, na, cols)),
-        ((na, nb, LANES),),
+        ((fibs * (4 * per + 1), LANES), (tiles, nb * na, LANES)),
+        ((na, nb, LANES), (tiles, nb, na, LANES), (nb, na)),
+        copies=tiles + 1,
+        far_in=(0, 1),
     )
     packets = swap(packets, "fib", fibs)
     (answers,) = call(
@@ -281,7 +312,15 @@
         functools.partial(coarse_kernel, lvls, nb, tiles), "coarse_b", (packets,), ((lvls * 3 * tiles, LANES),)
     )
     answers = swap(answers, "lvl", lvls)
-    (out,) = call(functools.partial(last_kernel, lvls), "last", (answers, fine), ((nb, na, cols),))
+    (out,) = call(
+        functools.partial(last_kernel, lvls),
+        "last",
+        (answers, fine),
+        ((nb, na, cols),),
+        ((CHUNKS, nb // CHUNKS, na, cols),),
+        copies=CHUNKS,
+        far_out=(0,),
+    )
     return out
 
 

time: 79.5 us -> 78.4 us (0.986)
  local copies, waits for them, and re-layouts: 1.92 us -> 0.01 us
  Pallas kernels: 2.72 us -> 3.62 us
    unnamed x4 -> x2, local copies, waits for them, and re-layouts: 1.92 us -> 0.01 us
    pallas_call x5, Pallas kernels: 2.72 us -> 3.62 us  [call(): pl.pallas_call(body, name=name, out_shape=[jax.ShapeDtypeStruct(shape, jn...]
where the time goes in v2:
time: 78.4 us; the launch traced here: 78.2 us
  blocking collectives  74.5 us (95%)
  Pallas kernels  3.62 us (5%)
    all_to_all x4, blocking collectives, swap(): return lax.all_to_all(apart, axis, 0, 0).reshape(packets.shape)  74.5 us
    pallas_call x5, Pallas kernels, call(): pl.pallas_call(body, name=name, out_shape=[jax.ShapeDtypeStruct(shape, jn...  3.62 us

profile of v2, /device:TPU:1, one launch (start us, length us, event | category | flops | bytes accessed | tf_op | source)
XLA Modules:
  0.0 78.2 jit_solution(16644314620813489672)
XLA Ops:
  0.0 1.8 %first.1 = (f32[544,128]{1,0:T(8,128)S(1)}, f32[8,256,128]{2,1,0:T(8,128)S(1)}) custom-call(f32[16,16,1024]{2,1,0:T(8,128)} %values_ref.1, f32[16,16]{1,0:T(8,128)} %vol_ref.3), custom_call_target="tpu_custom_call" | custom-call | tf_op jit(solution)/shard_map/first/pallas_call | solution.py:268
  1.8 22.1 %all_to_all.20 = f32[32,17,1,128]{3,2,1,0:T(1,128)S(1)} all-to-all(f32[32,17,1,128]{3,2,1,0:T(1,128)S(1)} %bitcast.16), channel_id=1, replica_groups=mesh['lvl'=16,'fib'=32] {'fib'}, dimensions={0} | all-to-all | bytes 557056 | tf_op jit(solution)/shard_map/all_to_all | solution.py:281
  23.9 0.2 coarse_a.1
  24.0 0.0 copy-start
  24.1 14.1 %all_to_all.21 = f32[32,12,1,128]{3,2,1,0:T(1,128)S(1)} all-to-all(f32[32,12,1,128]{3,2,1,0:T(1,128)S(1)} %bitcast.15), channel_id=1, replica_groups=mesh['lvl'=16,'fib'=32] {'fib'}, dimensions={0} | all-to-all | bytes 393216 | tf_op jit(solution)/shard_map/all_to_all | solution.py:281
  38.2 0.0 copy-done
  38.2 0.6 second.1
  38.8 25.2 %all_to_all.22 = f32[16,33,1,128]{3,2,1,0:T(1,128)S(1)} all-to-all(f32[16,33,1,128]{3,2,1,0:T(1,128)S(1)} %bitcast.17), channel_id=1, replica_groups=mesh['lvl'=16,'fib'=32] {'lvl'}, dimensions={0} | all-to-all | bytes 540672 | tf_op jit(solution)/shard_map/all_to_all | solution.py:281
  64.0 0.1 coarse_b.1
  64.1 13.0 %all_to_all.23 = f32[16,24,1,128]{3,1,2,0:T(8,128)S(1)} all-to-all(f32[16,24,1,128]{3,1,2,0:T(8,128)S(1)} %bitcast.14), channel_id=1, replica_groups=mesh['lvl'=16,'fib'=32] {'lvl'}, dimensions={0} | all-to-all | bytes 393216 | tf_op jit(solution)/shard_map/all_to_all | solution.py:281
  77.1 1.1 %last.1 = f32[16,16,1024]{2,1,0:T(8,128)} custom-call(f32[384,128]{1,0:T(8,128)S(1)} %bitcast.13, f32[16,16,1024]{2,1,0:T(8,128)S(1)} %get-tuple-element.12.fine_ref), custom_call_target="tpu_custom_call" | custom-call | tf_op jit(solution)/shard_map/last/pallas_call | solution.py:268
Async XLA Ops:
  24.0 14.2 %copy-start = (f32[16,16]{1,0:T(8,128)S(1)}, f32[16,16]{1,0:T(8,128)}, u32[]{:S(2)}) copy-start(f32[16,16]{1,0:T(8,128)} %vol_ref.3) | copy-start | bytes 3076

commit v3 on v2

--- a/solution.py
+++ b/solution.py
@@ -118,7 +118,9 @@
             tilt = (2.0 / n) * (before_beta * right0 + slope * right3)
             lower = SIDE + beta - kappa
             own = own + lower * (1.0 - 1.0 / n) + (LINEAR * right2 - tilt)
-            dual = dual + rights[i - 1] + lower * lasts[i - 1]
+            dual = dual + rights[i - 1]
+            if lasts is not None:
+                dual = dual + lower * lasts[i - 1]
             dual = dual + (lower * (1.0 / n) + (LINEAR * right1 + tilt)) * node[i - 1]
         duals.append(dual + own * node[i])
     sums = ascend(duals)
@@ -168,13 +170,13 @@
             packet_ref[pl.ds(start, nb, stride=stride), :] = quad
 
 
-def coarse_kernel(count, n, per, packet_ref, answer_ref):
-    rows = 4 * per + 1
+def coarse_kernel(count, n, per, kinds, packet_ref, answer_ref):
+    rows = kinds * per + 1
 
     def piece(i, q):
         return packet_ref[i * rows + q * per : i * rows + (q + 1) * per, :]
 
-    quads = [[piece(i, q) for i in range(count)] for q in range(4)]
+    quads = [[piece(i, q) for i in range(count)] if q < kinds else None for q in range(4)]
     kappas = [packet_ref[(i + 1) * rows - 1 : (i + 1) * rows, :] for i in range(count)]
     node, outs = coarse_pass(*quads, kappas, n)
     for i in range(count):
@@ -186,7 +188,7 @@
         answer_ref[base + 2 * per : base + 3 * per, :] = outs[i]
 
 
-def second_kernel(fib_count, lvl_count, answer_ref, fine_ref, vol_ref, packet_ref, next_ref, kappa_ref):
+def second_kernel(fib_count, lvl_count, answer_ref, fine_ref, vol_ref, next_vol_ref, packet_ref, next_ref, kappa_ref):
     n, na, _ = next_ref.shape
     tiles = fine_ref.shape[0]
     fib_total = na * fib_count
@@ -198,9 +200,10 @@
     diagonal = lax.broadcasted_iota(jnp.int32, (na, na), 0) == lax.broadcasted_iota(
         jnp.int32, (na, na), 1
     )
-    for r in range(n):
+    for r in range(n + 1):
         place = index * (1.0 / lvl_count) + r / total
-        column = jnp.sum(jnp.where(diagonal, vol[r : r + 1, :], 0.0), axis=1, keepdims=True)
+        row = next_vol_ref[0:1, :] if r == n else vol[r : r + 1, :]
+        column = jnp.sum(jnp.where(diagonal, row, 0.0), axis=1, keepdims=True)
         root = column * place
         kappa_ref[r] = jnp.broadcast_to((KAPPA_SCALE * 0.5) * root * root, (na, LANES))
     at = lax.broadcasted_iota(jnp.int32, (na, LANES), 0)
@@ -211,7 +214,8 @@
     high = LINEAR * share - tilt
     parts = fib_count // n
     per = tiles // parts
-    rows = 4 * tiles + 1
+    rows = 3 * tiles + 1
+    next_lower = SIDE + (first_beta + DRIFT / lvl_count) - kappa_ref[n]
     packet_ref[pl.ds(rows - 1, na, stride=rows), :] = kappa_ref[0]
     for t in range(tiles):
         lanes = slice(t * LANES, (t + 1) * LANES)
@@ -223,11 +227,11 @@
             head = answer_ref[base + 2 * per : base + 2 * per + 1, :]
             body = fine_ref[t, b * na : (b + 1) * na, :] + low * own + high * following
             block.append(jnp.where(is_head, head, body))
-        fine, quads = local_pass(block, lambda r: kappa_ref[r], first_beta, total)
+        fine, (first, left, right, final) = local_pass(block, lambda r: kappa_ref[r], first_beta, total)
         for r in range(1, n):
             next_ref[r, :, lanes] = fine[r - 1]
-        for q, quad in enumerate(quads):
-            packet_ref[pl.ds(q * tiles + t, na, stride=rows), :] = quad
+        for q, row in enumerate((first, left, right + next_lower * final)):
+            packet_ref[pl.ds(q * tiles + t, na, stride=rows), :] = row
 
 
 def last_kernel(count, answer_ref, fine_ref, out_ref, stage_ref, sems):
@@ -286,6 +290,7 @@
     fibs, lvls = lax.axis_size("fib"), lax.axis_size("lvl")
     tiles = cols // LANES
     per = tiles * nb // fibs
+    next_vol = lax.ppermute(local_vol, "lvl", [(i + 1, i) for i in range(lvls - 1)])
     packets, fine = call(
         functools.partial(first_kernel, fibs),
         "first",
@@ -297,19 +302,19 @@
     )
     packets = swap(packets, "fib", fibs)
     (answers,) = call(
-        functools.partial(coarse_kernel, fibs, na, per), "coarse_a", (packets,), ((fibs * 3 * per, LANES),)
+        functools.partial(coarse_kernel, fibs, na, per, 4), "coarse_a", (packets,), ((fibs * 3 * per, LANES),)
     )
     answers = swap(answers, "fib", fibs)
     packets, fine = call(
         functools.partial(second_kernel, fibs, lvls),
         "second",
-        (answers, fine, local_vol),
-        ((lvls * (4 * tiles + 1), LANES), (nb, na, cols)),
-        ((nb, na, LANES),),
+        (answers, fine, local_vol, next_vol),
+        ((lvls * (3 * tiles + 1), LANES), (nb, na, cols)),
+        ((nb + 1, na, LANES),),
     )
     packets = swap(packets, "lvl", lvls)
     (answers,) = call(
-        functools.partial(coarse_kernel, lvls, nb, tiles), "coarse_b", (packets,), ((lvls * 3 * tiles, LANES),)
+        functools.partial(coarse_kernel, lvls, nb, tiles, 3), "coarse_b", (packets,), ((lvls * 3 * tiles, LANES),)
     )
     answers = swap(answers, "lvl", lvls)
     (out,) = call(

time: 78.4 us -> 78.1 us (level)
  blocking collectives: 74.5 us -> 59 us
  starting transfers between devices: 0 us -> 8.31 us
  waiting for transfers between devices: 0 us -> 6.14 us
    all_to_all x4 -> x3, blocking collectives: 74.5 us -> 59 us  [swap(): return lax.all_to_all(apart, axis, 0, 0).reshape(packets.shape)]
    all_to_all x0 -> x1, starting transfers between devices: none -> 4.59 us  [swap(): return lax.all_to_all(apart, axis, 0, 0).reshape(packets.shape)]
    ppermute x0 -> x1, starting transfers between devices: none -> 3.72 us  [per_device(): lax.ppermute(local_vol, 'lvl', [(i + 1, i) for i in range(lvls - 1)])]
    ppermute x0 -> x1, waiting for transfers between devices: none -> 3.59 us  [per_device(): lax.ppermute(local_vol, 'lvl', [(i + 1, i) for i in range(lvls - 1)])]
    all_to_all x0 -> x1, waiting for transfers between devices: none -> 2.55 us  [swap(): return lax.all_to_all(apart, axis, 0, 0).reshape(packets.shape)]
  transfers between devices with their start and end apart: 0 -> 2, of which waited for: 0 -> 2; matrix products, arithmetic and copies ran while one was open for 0% -> 0% of each run, Pallas kernels for 0% -> 0%
where the time goes in v3:
time: 78.1 us; the launch traced here: 77.7 us
  blocking collectives  59 us (76%)
  starting transfers between devices  8.31 us (11%)
  waiting for transfers between devices  6.14 us (8%)
  Pallas kernels  4.26 us (5%)
    all_to_all x3, blocking collectives, swap(): return lax.all_to_all(apart, axis, 0, 0).reshape(packets.shape)  59 us
    all_to_all x1, starting transfers between devices, swap(): return lax.all_to_all(apart, axis, 0, 0).reshape(packets.shape)  4.59 us
    pallas_call x5, Pallas kernels, call(): pl.pallas_call(body, name=name, out_shape=[jax.ShapeDtypeStruct(shape, jn...  4.26 us
    ppermute x1, starting transfers between devices, per_device(): lax.ppermute(local_vol, 'lvl', [(i + 1, i) for i in range(lvls - 1)])  3.72 us
    ppermute x1, waiting for transfers between devices, per_device(): lax.ppermute(local_vol, 'lvl', [(i + 1, i) for i in range(lvls - 1)])  3.59 us
    all_to_all x1, waiting for transfers between devices, swap(): return lax.all_to_all(apart, axis, 0, 0).reshape(packets.shape)  2.55 us
  transfers between devices with their start and end apart: 2, of which 2 were waited for; matrix products, arithmetic and copies ran while one was open for 0% of the time, Pallas kernels for 0%

profile of v3, /device:TPU:1, one launch (start us, length us, event | category | flops | bytes accessed | tf_op | source)
XLA Modules:
  0.0 77.7 jit_solution(6801499177932244605)
XLA Ops:
  0.0 1.8 %first.1 = (f32[544,128]{1,0:T(8,128)S(1)}, f32[8,256,128]{2,1,0:T(8,128)S(1)}) custom-call(f32[16,16,1024]{2,1,0:T(8,128)} %values_ref.1, f32[16,16]{1,0:T(8,128)} %vol_ref.3), custom_call_target="tpu_custom_call" | custom-call | tf_op jit(solution)/shard_map/first/pallas_call | solution.py:272
  1.8 22.1 %all_to_all.20 = f32[32,17,1,128]{3,2,1,0:T(1,128)S(1)} all-to-all(f32[32,17,1,128]{3,2,1,0:T(1,128)S(1)} %bitcast.15), channel_id=1, replica_groups=mesh['lvl'=16,'fib'=32] {'fib'}, dimensions={0} | all-to-all | bytes 557056 | tf_op jit(solution)/shard_map/all_to_all | solution.py:285
  23.9 0.8 %coarse_a.1 = f32[384,128]{1,0:T(8,128)} custom-call(f32[544,128]{1,0:T(8,128)S(1)} %bitcast.10), custom_call_target="tpu_custom_call" | custom-call | tf_op jit(solution)/shard_map/coarse_a/pallas_call | solution.py:272
  24.7 0.0 copy-start
  24.7 4.6 %all-to-all-start.1 = ((f32[32,12,1,128]{3,2,1,0:T(1,128)}), f32[32,12,1,128]{3,2,1,0:T(1,128)S(1)}, u32[]{:S(2)}, u32[]{:S(2)}) async-start(f32[32,12,1,128]{3,2,1,0:T(1,128)} %bitcast.2), calls=%async_computation.1 | async-start | bytes 393216 | tf_op jit(solution)/shard_map/all_to_all | solution.py:285
  29.3 0.0 copy-done
  29.3 3.7 %collective-permute-start = (f32[16,16]{1,0:T(8,128)S(1)}, f32[16,16]{1,0:T(8,128)S(1)}, u32[]{:S(2)}, u32[]{:S(2)}) collective-permute-start(f32[16,16]{1,0:T(8,128)S(1)} %copy-done), channel_id=1, source_target_pairs={{32,0},{64,32},{96,64},{128,96},{160,128},{192,160},{224,192},{256... | collective-permute-start | bytes 3080 | tf_op jit(solution)/shard_map/ppermute | solution.py:293
  33.1 3.6 %collective-permute-done.next_vol_ref = f32[16,16]{1,0:T(8,128)S(1)} collective-permute-done((f32[16,16]{1,0:T(8,128)S(1)}, f32[16,16]{1,0:T(8,128)S(1)}, u32[]{:S(2)}, u32[]{:S(2)}) %collective-permute-start) | collective-permute-done | bytes 1056 | tf_op jit(solution)/shard_map/ppermute | solution.py:293
  36.6 2.6 %all-to-all-done.1 = f32[32,12,1,128]{3,2,1,0:T(1,128)S(1)} async-done(((f32[32,12,1,128]{3,2,1,0:T(1,128)}), f32[32,12,1,128]{3,2,1,0:T(1,128)S(1)}, u32[]{:S(2)}, u32[]{:S(2)}) %all-to-all-start.1) | async-done | bytes 196640 | tf_op jit(solution)/shard_map/all_to_all | solution.py:285
  39.2 0.6 second.1
  39.8 23.8 %all_to_all.21 = f32[16,25,1,128]{3,2,1,0:T(1,128)S(1)} all-to-all(f32[16,25,1,128]{3,2,1,0:T(1,128)S(1)} %bitcast.16), channel_id=1, replica_groups=mesh['lvl'=16,'fib'=32] {'lvl'}, dimensions={0} | all-to-all | bytes 409600 | tf_op jit(solution)/shard_map/all_to_all | solution.py:285
  63.6 0.1 coarse_b.1
  63.7 13.0 %all_to_all.22 = f32[16,24,1,128]{3,1,2,0:T(8,128)S(1)} all-to-all(f32[16,24,1,128]{3,1,2,0:T(8,128)S(1)} %bitcast.14), channel_id=1, replica_groups=mesh['lvl'=16,'fib'=32] {'lvl'}, dimensions={0} | all-to-all | bytes 393216 | tf_op jit(solution)/shard_map/all_to_all | solution.py:285
  76.7 1.1 %last.1 = f32[16,16,1024]{2,1,0:T(8,128)} custom-call(f32[384,128]{1,0:T(8,128)S(1)} %bitcast.13, f32[16,16,1024]{2,1,0:T(8,128)S(1)} %get-tuple-element.12.fine_ref), custom_call_target="tpu_custom_call" | custom-call | tf_op jit(solution)/shard_map/last/pallas_call | solution.py:272
Async XLA Ops:
  24.7 4.6 %copy-start = (f32[16,16]{1,0:T(8,128)S(1)}, f32[16,16]{1,0:T(8,128)}, u32[]{:S(2)}) copy-start(f32[16,16]{1,0:T(8,128)} %vol_ref.3) | copy-start | bytes 3076
  24.7 14.5 %all-to-all-start.1 = ((f32[32,12,1,128]{3,2,1,0:T(1,128)}), f32[32,12,1,128]{3,2,1,0:T(1,128)S(1)}, u32[]{:S(2)}, u32[]{:S(2)}) async-start(f32[32,12,1,128]{3,2,1,0:T(1,128)} %bitcast.2), calls=%async_computation.1 | async-start | bytes 393216 | tf_op jit(solution)/shard_map/all_to_all | solution.py:285
  29.3 7.3 %collective-permute-start = (f32[16,16]{1,0:T(8,128)S(1)}, f32[16,16]{1,0:T(8,128)S(1)}, u32[]{:S(2)}, u32[]{:S(2)}) collective-permute-start(f32[16,16]{1,0:T(8,128)S(1)} %copy-done), channel_id=1, source_target_pairs={{32,0},{64,32},{96,64},{128,96},{160,128},{192,160},{224,192},{256... | collective-permute-start | bytes 3080 | tf_op jit(solution)/shard_map/ppermute | solution.py:293

commit v4 on v2

--- a/solution.py
+++ b/solution.py
@@ -157,8 +157,8 @@
         packet_ref[pl.ds(part * rows + rows - 1, nb, stride=stride), :] = kappa_ref[0]
     for t in range(tiles):
         copies[t].wait()
-        tile = stage_ref.at[t].reshape(nb * n, LANES)
-        block = [tile[pl.ds(r, nb, stride=n), :] for r in range(n)]
+        turned = jnp.swapaxes(stage_ref[t], 0, 1)
+        block = [turned[r] for r in range(n)]
         fine, quads = local_pass(block, lambda r: kappa_ref[r], first_beta, total)
         fine_ref[t, pl.ds(0, nb, stride=n), :] = jnp.zeros_like(fine[0])
         for r in range(1, n):

time: 78.4 us -> 78.4 us (level)
  no operation moved by 1% of the time
where the time goes in v4:
time: 78.4 us; the launch traced here: 78.1 us
  blocking collectives  74.5 us (95%)
  Pallas kernels  3.54 us (5%)
    all_to_all x4, blocking collectives, swap(): return lax.all_to_all(apart, axis, 0, 0).reshape(packets.shape)  74.5 us
    pallas_call x5, Pallas kernels, call(): pl.pallas_call(body, name=name, out_shape=[jax.ShapeDtypeStruct(shape, jn...  3.54 us

profile of v4, /device:TPU:1, one launch (start us, length us, event | category | flops | bytes accessed | tf_op | source)
XLA Modules:
  0.0 78.1 jit_solution(14123731946937796132)
XLA Ops:
  0.0 1.7 %first.1 = (f32[544,128]{1,0:T(8,128)S(1)}, f32[8,256,128]{2,1,0:T(8,128)S(1)}) custom-call(f32[16,16,1024]{2,1,0:T(8,128)} %values_ref.1, f32[16,16]{1,0:T(8,128)} %vol_ref.3), custom_call_target="tpu_custom_call" | custom-call | tf_op jit(solution)/shard_map/first/pallas_call | solution.py:268
  1.7 22.1 %all_to_all.20 = f32[32,17,1,128]{3,2,1,0:T(1,128)S(1)} all-to-all(f32[32,17,1,128]{3,2,1,0:T(1,128)S(1)} %bitcast.16), channel_id=1, replica_groups=mesh['lvl'=16,'fib'=32] {'fib'}, dimensions={0} | all-to-all | bytes 557056 | tf_op jit(solution)/shard_map/all_to_all | solution.py:281
  23.8 0.2 coarse_a.1
  24.0 0.0 copy-start
  24.0 14.1 %all_to_all.21 = f32[32,12,1,128]{3,2,1,0:T(1,128)S(1)} all-to-all(f32[32,12,1,128]{3,2,1,0:T(1,128)S(1)} %bitcast.15), channel_id=1, replica_groups=mesh['lvl'=16,'fib'=32] {'fib'}, dimensions={0} | all-to-all | bytes 393216 | tf_op jit(solution)/shard_map/all_to_all | solution.py:281
  38.1 0.0 copy-done
  38.1 0.6 second.1
  38.7 25.2 %all_to_all.22 = f32[16,33,1,128]{3,2,1,0:T(1,128)S(1)} all-to-all(f32[16,33,1,128]{3,2,1,0:T(1,128)S(1)} %bitcast.17), channel_id=1, replica_groups=mesh['lvl'=16,'fib'=32] {'lvl'}, dimensions={0} | all-to-all | bytes 540672 | tf_op jit(solution)/shard_map/all_to_all | solution.py:281
  63.9 0.1 coarse_b.1
  64.0 13.0 %all_to_all.23 = f32[16,24,1,128]{3,1,2,0:T(8,128)S(1)} all-to-all(f32[16,24,1,128]{3,1,2,0:T(8,128)S(1)} %bitcast.14), channel_id=1, replica_groups=mesh['lvl'=16,'fib'=32] {'lvl'}, dimensions={0} | all-to-all | bytes 393216 | tf_op jit(solution)/shard_map/all_to_all | solution.py:281
  77.0 1.1 %last.1 = f32[16,16,1024]{2,1,0:T(8,128)} custom-call(f32[384,128]{1,0:T(8,128)S(1)} %bitcast.13, f32[16,16,1024]{2,1,0:T(8,128)S(1)} %get-tuple-element.12.fine_ref), custom_call_target="tpu_custom_call" | custom-call | tf_op jit(solution)/shard_map/last/pallas_call | solution.py:268
Async XLA Ops:
  24.0 14.2 %copy-start = (f32[16,16]{1,0:T(8,128)S(1)}, f32[16,16]{1,0:T(8,128)}, u32[]{:S(2)}) copy-start(f32[16,16]{1,0:T(8,128)} %vol_ref.3) | copy-start | bytes 3076
